TPU v7x, 512 devices: a whole 4x4x16 slice. The times are simulated.
512 devices in a mesh: ex: 64 (over y, z_lo, core), coord: 8 (over z_hi, x).
Axes of the slice: x: 4, y: 4, z: 16 (z_hi: 2, z_lo: 8; z = z_hi * 8 + z_lo), core: 2. Of those that a mesh axis runs over, the one named last changes fastest.
Arguments:
- cotangent: bfloat16 [2048, 64, 4096], P('ex', None, 'coord'), may hold values from -0.19921875 to 0.19921875
- low_acts: bfloat16 [2048, 64, 64], P('ex'), may hold values from -6 to 6
- sign_bits: int32 [4096, 3], P('coord'), may hold values from 0 to 1073741823
- sample_blocks: int32 [64], replicated, may hold values from 0 to 2047, as said below
- bank: bfloat16 [512, 8192], P('ex', 'coord'), may hold values from -6 to 6
- target_ids: int32 [256], replicated, may hold values from 0 to 511, as said below
Outputs:
- sketches: bfloat16 [2048, 8192], P('ex', 'coord')
- scores: float32 [2048, 256], P('ex')
Inputs may be any that keep to these rules, and one draw needn't show every extreme that they name: `sample_blocks`: distinct block numbers. `target_ids`: every aligned block of 8 bank rows is named by at least one id; ids may repeat, and how many rows of a block are named varies from block to block.
All inputs are finite; a program needn't handle non-finite values.
Results may differ from a plain program's by a relative error of at most 0.0049.
Values may be sent and summed in bfloat16 or wider, within the bound.
A program may use at most 64 MiB of HBM per device.

v0:
```python
import math

import jax
import jax.numpy as jnp
import numpy as np
from jax import lax
from jax.sharding import PartitionSpec as P


def parity_sign(left, right):
    both = jnp.bitwise_and(left, right)
    parity = jnp.zeros_like(both)
    for bit_pos in range(24):
        parity = jnp.bitwise_xor(parity, jnp.bitwise_and(jnp.right_shift(both, bit_pos), 1))
    return (1 - 2 * parity).astype(jnp.float32)


def unpack_signs(sign_bits, rank):
    ranks = np.arange(rank)
    words = sign_bits[:, ranks // 30]
    shifted = jnp.right_shift(words, jnp.asarray(ranks % 30, jnp.int32)[None, :])
    return (1 - 2 * jnp.bitwise_and(shifted, 1)).astype(jnp.float32)


def body(cotangent, low_acts, sign_bits, sample_blocks, bank, target_ids):
    ex_rows, tok_count, dout_dev = cotangent.shape
    rank = low_acts.shape[2]
    local_len = dout_dev * rank
    block_count = sample_blocks.shape[0]
    sketch_len = block_count * 128
    coord_pos = lax.axis_index("coord")
    coord_count = lax.axis_size("coord")
    grads = jnp.einsum("etd,etr->edr", cotangent, low_acts, preferred_element_type=jnp.float32)
    signs = unpack_signs(sign_bits, rank)
    signed = (grads * signs[None]).astype(jnp.bfloat16)
    per_block = 128 // rank
    within = sample_blocks % (local_len // 128)
    owner = sample_blocks // (local_len // 128)
    row_sel = (
        per_block * within[:, None] + jnp.arange(per_block, dtype=jnp.int32)[None, :]
    ).reshape(-1)
    out_pos = jnp.arange(dout_dev, dtype=jnp.int32)
    rank_pos = jnp.arange(rank, dtype=jnp.int32)
    small_had = parity_sign(rank_pos[:, None], rank_pos[None, :])
    full_had = parity_sign(out_pos[:, None], out_pos[None, :]).astype(jnp.bfloat16)
    whole = jnp.einsum("mo,eor->emr", full_had, signed, preferred_element_type=jnp.float32)
    first = jnp.take(whole, row_sel, axis=1)
    second = jnp.einsum("emr,sr->ems", first, small_had, precision=lax.Precision.HIGHEST)
    dev_sign = parity_sign(owner, coord_pos) * (1.0 / math.sqrt(sketch_len))
    share_len = sketch_len // coord_count
    weighted = second.reshape(ex_rows, block_count, 128) * dev_sign[None, :, None]
    term_rows = jnp.swapaxes(weighted.reshape(ex_rows, coord_count, share_len), 0, 1).reshape(
        coord_count * ex_rows, share_len
    )
    share = lax.psum_scatter(term_rows, "coord", scatter_dimension=0, tiled=True)
    sketch = share.astype(jnp.bfloat16)
    piece = lax.all_gather(bank, "ex", axis=0, tiled=True)
    piece_rows = jnp.arange(piece.shape[0], dtype=jnp.int32)
    onehot = (target_ids[:, None] == piece_rows[None, :]).astype(jnp.bfloat16)
    chosen = jnp.dot(onehot, piece, preferred_element_type=jnp.float32)
    targets = chosen.astype(jnp.bfloat16)
    dots = jnp.einsum("ek,tk->et", sketch, targets, preferred_element_type=jnp.float32)
    sketch_f = sketch.astype(jnp.float32)
    target_f = targets.astype(jnp.float32)
    own_part = jnp.sum(sketch_f * sketch_f, axis=1)
    tnorm_part = jnp.sum(target_f * target_f, axis=1)
    dots, own, tnorm = lax.psum((dots, own_part, tnorm_part), "coord")
    scores = (
        math.sqrt(sketch_len)
        * dots
        * lax.rsqrt(own + 1e-06)[:, None]
        * lax.rsqrt(tnorm + 1e-06)[None, :]
    )
    return (sketch, scores)


def solution(mesh):
    in_specs = (
        P("ex", None, "coord"),
        P("ex", None, None),
        P("coord", None),
        P(),
        P("ex", "coord"),
        P(),
    )
    out_specs = (P("ex", "coord"), P("ex", None))
    return jax.shard_map(body, mesh=mesh, in_specs=in_specs, out_specs=out_specs, check_vma=False)
```

profile of v0, /device:TPU:8, one launch (start us, length us, event | category | flops | bytes accessed | tf_op | source)
XLA Modules:
  0.0 242.2 jit_solution(1931496328957011422)
XLA Ops:
  8.0 0.0 copy-start
  8.0 0.0 copy-start.2
  8.0 0.0 copy-start.3
  8.0 0.0 all-gather.2.cloned.1.call-start
  8.1 0.7 all-gather.2.cloned.1.call-update
  8.8 0.0 reduce-scatter.2.cloned.1.call-start
  8.8 0.7 pad_clamp_fusion.1
  9.5 0.7 fusion.131
  10.1 1.4 gather_fusion
  11.6 0.0 copy-done.2
  11.6 0.1 convert_bitcast_fusion
  11.7 0.0 copy-done
  11.7 0.0 copy-done.3
  11.7 6.1 %convolution_bitcast_fusion = f32[32,512,64]{1,2,0:T(8,128)} fusion(bf16[32,64,512]{2,1,0:T(8,128)(2,1)S(1)} %copy-done, bf16[32,64,64]{2,1,0:T(8,128)(2,1)S(1)} %copy-done.3, f32[512,64]{0,1:T(8,128)S(1)} %convert_bitcast_fusion), kind=kOutput, calls=%fused_computation.3 | convolution fusion | flops 1229979648 | bytes 6684672 | tf_op jit(solution)/shard_map/mo,eor->emr/dot_general | solution.py:46
  17.8 0.1 iota_add_fusion
  17.9 0.1 add.88
  18.0 0.1 add.84
  18.1 9.1 %copy.18 = f32[32,512,64]{2,0,1:T(8,128)} copy(f32[32,512,64]{1,2,0:T(8,128)} %convolution_bitcast_fusion) | data formatting | bytes 8388608 | tf_op jit(solution)/shard_map/mo,eor->emr/transpose | solution.py:46
  27.3 5.4 %gather_fusion.1 = f32[128,32,64]{2,1,0:T(8,128)} fusion(f32[32,512,64]{2,0,1:T(8,128)} %copy.18, s32[1024]{0:T(1024)S(1)} %pad_clamp_fusion), kind=kCustom, calls=%fused_computation.1 | custom fusion | bytes 2097664 | tf_op jit(solution)/shard_map/jit(_take)/gather | solution.py:47
  32.7 1.8 select_bitcast_fusion
  34.5 4.7 %fusion = f32[32,128,64]{2,1,0:T(8,128)} fusion(f32[32,128,64]{2,0,1:T(8,128)S(1)} %select_bitcast_fusion), kind=kOutput, calls=%fused_computation.4 | convolution fusion | flops 201633792 | bytes 2097152 | tf_op jit(solution)/shard_map/emr,sr->ems/dot_general | solution.py:48
  39.2 0.0 copy-start.5
  39.2 2.0 reshape.83
  41.3 0.0 copy-done.5
  41.3 0.1 mul.94
  41.4 0.1 copy.21
  41.5 0.1 broadcast_bitcast_fusion
  41.5 0.1 multiply_bitcast_fusion
  41.6 0.0 copy-start.4
  41.6 1.6 copy.22
  43.2 0.0 reduce-scatter.2.cloned.1.call-update
  43.2 93.5 %all-gather.2.cloned.1.call-done = bf16[512,1024]{1,0:T(8,128)(2,1)} async-done(((bf16[8,1024]{1,0:T(8,128)(2,1)}), bf16[512,1024]{1,0:T(8,128)(2,1)}) %all-gather.2.cloned.1.call-update) | async-done | bytes 1048592 | tf_op jit(solution)/shard_map/all_gather | solution.py:57
  136.7 0.0 copy-done.4
  136.7 1.8 multiply_reduce_fusion
  138.5 27.2 %reduce-scatter.2.cloned.1.call-done = f32[32,1024]{1,0:T(8,128)} async-done(((f32[256,1024]{1,0:T(8,128)}), f32[32,1024]{1,0:T(8,128)}) %reduce-scatter.2.cloned.1.call-update) | async-done | bytes 131088 | tf_op jit(solution)/shard_map/reduce_scatter | solution.py:55
  165.8 1.0 multiply_reduce_fusion.1
  166.8 0.0 copy-start.1
  166.8 0.2 fusion.181
  167.1 66.9 %all-reduce = (f32[32,256]{1,0:T(8,128)S(1)}, f32[256]{0:T(256)S(1)}, f32[32]{0:T(128)S(1)}) all-reduce(f32[32,256]{1,0:T(8,128)S(1)} %fusion.181, f32[256]{0:T(256)S(1)} %get-tuple-element.7, f32[32]{0:T(128)S(1)} %get-tuple-element.5), channel_id=1, replica_groups=mesh['ex'=64,'coord'=8] {'coord'}, use_global_device_ids=true, to_apply=%region_1.2 | all-reduce | flops 8480 | bytes 67840 | tf_op jit(solution)/shard_map/psum | solution.py:67
  234.0 0.7 multiply_multiply_fusion
  234.7 0.0 copy-done.1
  (6 shorter events, 0.1 us)
Async XLA Ops:
  8.0 3.7 %copy-start = (bf16[32,64,512]{2,1,0:T(8,128)(2,1)S(1)}, bf16[32,64,512]{2,1,0:T(8,128)(2,1)}, u32[]{:S(2)}) copy-start(bf16[32,64,512]{2,1,0:T(8,128)(2,1)} %param.9) | copy-start | bytes 6291460
  8.0 3.6 %copy-start.2 = (s32[64]{0:T(128)S(1)}, s32[64]{0:T(128)}, u32[]{:S(2)}) copy-start(s32[64]{0:T(128)} %constant.75.clone) | copy-start | bytes 772
  8.0 3.7 %copy-start.3 = (bf16[32,64,64]{2,1,0:T(8,128)(2,1)S(1)}, bf16[32,64,64]{2,1,0:T(8,128)(2,1)}, u32[]{:S(2)}) copy-start(bf16[32,64,64]{2,1,0:T(8,128)(2,1)} %param.10) | copy-start | bytes 786436
  8.0 128.7 %all-gather.2.cloned.1.call-start = ((), (), s32[]{:S(2)}) async-start(), calls=%async_computation.2 | async-start | bytes 1064960 | tf_op jit(solution)/shard_map/all_gather | solution.py:57
  8.8 157.0 %reduce-scatter.2.cloned.1.call-start = ((), (), s32[]{:S(2)}) async-start(), calls=%async_computation.1 | async-start | bytes 1179648 | tf_op jit(solution)/shard_map/reduce_scatter | solution.py:55
  39.2 2.0 copy-start.5
  41.6 95.1 %copy-start.4 = (s32[256]{0:T(256)S(1)}, s32[256]{0:T(256)}, u32[]{:S(2)}) copy-start(s32[256]{0:T(256)} %param.14) | copy-start | bytes 3076
  166.8 67.9 %copy-start.1 = (bf16[32,1024]{1,0:T(8,128)(2,1)}, bf16[32,1024]{1,0:T(8,128)(2,1)S(1)}, u32[]{:S(2)}) copy-start(bf16[32,1024]{1,0:T(8,128)(2,1)S(1)} %get-tuple-element.6) | copy-start | bytes 196612
Sparse Core Ops, SparseCore 0:
  11.2 125.4 all-gather.1
Sparse Core Ops, SparseCore 1:
  43.3 122.4 reduce-scatter.1
where the time goes:
time: 243 us; the launch traced here: 242 us
  waiting for transfers between devices  121 us (50%)
  blocking collectives  66.9 us (28%)
  local copies, waits for them, and re-layouts  20.1 us (8%)
  between operations  15.6 us (6%)
  matrix products  12.8 us (5%)
  other arithmetic  5.16 us (2%)
    all_gather x1, waiting for transfers between devices, body(): piece = lax.all_gather(bank, 'ex', axis=0, tiled=True)  93.5 us
    psum x1, blocking collectives, body(): dots, own, tnorm = lax.psum((dots, own_part, tnorm_part), 'coord')  66.9 us
    reduce_scatter x1, waiting for transfers between devices, body(): lax.psum_scatter(term_rows, 'coord', scatter_dimension=0, tiled=True)  27.2 us
    transpose x1, local copies, waits for them, and re-layouts, body(): jnp.einsum('mo,eor->emr', full_had, signed, preferred_element_type=jnp.fl...  9.12 us
    dot_general x1, matrix products, body(): jnp.einsum('mo,eor->emr', full_had, signed, preferred_element_type=jnp.fl...  6.09 us
    gather x1, local copies, waits for them, and re-layouts, body(): first = jnp.take(whole, row_sel, axis=1)  5.42 us
  transfers between devices with their start and end apart: 2, of which 2 were waited for; matrix products, arithmetic and copies ran while one was open for 15% of the time, Pallas kernels for 0%

commit v1 on v0

v1 whole, which is shorter than its diff:
```python
import functools
import math

import jax
import jax.numpy as jnp
from jax import lax
from jax.experimental import pallas as pl
from jax.experimental.pallas import tpu as pltpu
from jax.sharding import PartitionSpec as P

BF = jnp.bfloat16
F32 = jnp.float32
I32 = jnp.int32
MESH = pl.DeviceIdType.MESH

NX, NZH, NY, NZL, NCORE = 4, 2, 4, 8, 2
CHUNKS = 4
EX = 32
TOK = 64
RANK = 64
ODEV = 512
NSAMP = 64
NT = 256
SHARE = 1024
PAIRS = 4
COLS = PAIRS * 2 * RANK
MSG = 48


def xor(value, k):
    bit = 1
    while bit <= k:
        if k & bit:
            value = value + bit * (1 - 2 * ((value // bit) % 2))
        bit *= 2
    return value


def iota(shape, dim):
    return lax.broadcasted_iota(I32, shape, dim)


def parity_sign(v, bits):
    shift = 8
    while shift:
        if shift < bits:
            v = v ^ (v >> shift)
        shift //= 2
    return (1 - 2 * (v & 1)).astype(F32)


def dot(a, b, ca, cb):
    return lax.dot_general(a, b, (((ca,), (cb,)), ((), ())), preferred_element_type=F32)


def split(v):
    hi = v.astype(BF)
    return hi, (v - hi.astype(F32)).astype(BF)


def kernel(
    cot_hbm, low_hbm, sign_hbm, samp_hbm, bank_hbm, ids_hbm,
    sketch_ref, scores_ref,
    cot, low, sign, samp, bank, ids,
    st, had, part, xs, xr, own, zs, zr, ytmp, gath, targ, msg, mrx, mzs, mzr,
    in_sem, xs_sem, xr_sem, zs_sem, zr_sem, ls_sem, lr_sem, ys_sem, yr_sem,
    ms_sem, mr_sem, fs_sem, fr_sem,
):
    ex, co = lax.axis_index("ex"), lax.axis_index("coord")
    c, zl, y = ex % 2, (ex // 2) % NZL, ex // (2 * NZL)
    x, zh = co % NX, co // NX

    def dev_x(k):
        return (ex, zh * NX + xor(x, k))

    dev_zh = (ex, (1 - zh) * NX + x)

    def dev_zl(k):
        return ((y * NZL + xor(zl, k)) * 2 + c, co)

    def dev_yc(yk, ck):
        return ((xor(y, yk) * NZL + zl) * 2 + xor(c, ck), co)

    barrier = pltpu.get_barrier_semaphore()
    yc = [(yk, ck) for yk in range(NY) for ck in range(2) if yk or ck]
    partners = [dev_zh] + [dev_zl(k) for k in range(NZL - 1, 0, -1)]
    partners += [dev_x(k) for k in range(1, NX)] + [dev_yc(*p) for p in yc]
    for p in partners:
        pl.semaphore_signal(barrier, inc=1, device_id=p, device_id_type=MESH)

    loads = [
        pltpu.make_async_copy(src, dst, in_sem.at[n])
        for n, (src, dst) in enumerate(
            [(samp_hbm, samp), (sign_hbm, sign), (low_hbm, low), (bank_hbm, bank), (ids_hbm, ids), (cot_hbm, cot)]
        )
    ]
    for load in loads:
        load.start()

    loads[0].wait()
    rho = iota((128, 1), 0)
    share = (zh ^ ((rho // 16) % 2)) * NX + (x ^ (rho // 32))
    block = share * 8 + (rho % 16) // 2
    picked = jnp.where(iota((128, NSAMP), 1) == block, samp[...].astype(F32), 0.0)
    row = jnp.sum(picked, axis=1, keepdims=True).astype(I32) * 2 + rho % 2
    had[...] = parity_sign(row & (co * ODEV + iota((128, ODEV), 1)), 12).astype(BF)

    loads[1].wait()
    r = iota((RANK, 1), 0)
    word = jnp.where(r < 30, sign[0:1, :], jnp.where(r < 60, sign[1:2, :], sign[2:3, :]))
    shift = jnp.where(r < 30, r, jnp.where(r < 60, r - 30, r - 60))
    signs = (1 - 2 * ((word >> shift) & 1)).astype(F32)

    loads[2].wait()
    loads[3].wait()
    gath[0, 0] = jnp.concatenate([bank[:, :512], bank[:, 512:]], axis=0)
    loads[4].wait()
    loads[5].wait()

    def compute(n, _):
        for q in range(PAIRS):
            for e2 in range(2):
                e = e2 * 16 + n * PAIRS + q
                grad = dot(low[e], cot[e], 0, 0)
                at = (q * 2 + e2) * RANK
                st[at : at + RANK, :] = (grad * signs).astype(BF)
        res = dot(had[...], st[...], 1, 1)
        part[n] = res[:32]
        for k in range(1, NX):
            xs[n, k - 1] = res[32 * k : 32 * k + 32].astype(BF)
        return 0

    lax.fori_loop(0, CHUNKS, compute, 0)

    pl.semaphore_wait(barrier, len(partners))

    def remote(src, dst, ssem, rsem, to):
        return pltpu.make_async_remote_copy(
            src_ref=src, dst_ref=dst, send_sem=ssem, recv_sem=rsem, device_id=to, device_id_type=MESH
        )

    def x_copy(n, k):
        return remote(xs.at[n, k - 1], xr.at[n, k - 1], xs_sem.at[n, k - 1], xr_sem.at[n, k - 1], dev_x(k))

    def z_copy(n):
        return remote(zs.at[n], zr.at[n], zs_sem.at[n], zr_sem.at[n], dev_zh)

    def zl_copy(k):
        return remote(gath.at[0, 0], gath.at[0, k], ls_sem.at[k - 1], lr_sem.at[k - 1], dev_zl(k))

    def yc_copy(g, j):
        yk, ck = yc[j]
        four = pl.ds(g * 4, 4)
        return remote(gath.at[0, four], gath.at[j + 1, four], ys_sem.at[g, j], yr_sem.at[g, j], dev_yc(yk, ck))

    for k in (2, 1, 3):
        x_copy(0, k).start()
    for k in range(NZL - 1, 0, -1):
        zl_copy(k).start()
    for n in range(1, CHUNKS):
        for k in (2, 1, 3):
            x_copy(n, k).start()

    def x_done(n):
        for k in range(1, NX):
            x_copy(n, k).wait_recv()
        total = part[n] + xr[n, 0].astype(F32) + (xr[n, 1].astype(F32) + xr[n, 2].astype(F32))
        own[n] = total[:16]
        zs[n] = total[16:].astype(BF)
        z_copy(n).start()

    def forward(g, first):
        for k in range(first, g * 4 + 4):
            zl_copy(k).wait_recv()
        for j in range(len(yc) - 1, -1, -1):
            yc_copy(g, j).start()

    x_done(0)
    x_done(1)
    forward(0, 1)
    x_done(2)
    x_done(3)
    forward(1, 4)

    def pick(g):
        for j in range(len(yc)):
            yc_copy(g, j).wait_recv()
        rows = 8 * 64
        lane = iota((rows, 1), 0)
        i, half, slot = lane % 8, (lane // 8) % 2, lane // 16
        zk, ck, yk = slot % 4 + 4 * g, (slot // 4) % 2, slot // 8
        source = ((y ^ yk) * NZL + (zl ^ zk)) * 2 + (c ^ ck)
        match = (source * 8 + i) == ids[...]
        held = gath[:, g * 4 : g * 4 + 4].reshape(rows, 512)
        for h in range(2):
            onehot = jnp.where(match & (half == h), 1.0, 0.0).astype(BF)
            got = dot(onehot, held, 0, 0)
            if g == 0:
                targ[h] = got.astype(BF)
            else:
                targ[h] = (targ[h].astype(F32) + got).astype(BF)

    pick(0)

    a, b = iota((128, 128), 0), iota((128, 128), 1)
    small = jnp.where((a // 64) == (b // 64), parity_sign(a & b & 63, 6), 0.0).astype(BF)
    for n in range(CHUNKS):
        z_copy(n).wait_recv()
        total = own[n] + zr[n].astype(F32)
        lanes = jnp.concatenate([total[:, q * 128 : q * 128 + 128] for q in range(PAIRS)], axis=0)
        hi, lo = split(lanes)
        ytmp[n * 64 : n * 64 + 64, :] = (dot(hi, small, 1, 0) + dot(lo, small, 1, 0)) * (1.0 / math.sqrt(8192.0))
    left = iota((16, 128), 1) < 64
    for mp in range(8):
        even = ytmp[pl.ds(2 * mp, 16, stride=16), :]
        odd = ytmp[pl.ds(2 * mp + 1, 16, stride=16), :]
        top = jnp.where(left, even, pltpu.roll(odd, 64, 1))
        low_half = jnp.where(left, pltpu.roll(even, 64, 1), odd)
        sketch_ref[0:16, mp * 128 : mp * 128 + 128] = top.astype(BF)
        sketch_ref[16:32, mp * 128 : mp * 128 + 128] = low_half.astype(BF)

    ones = jnp.ones((8, 512), BF)

    def norms(values):
        v = values.astype(F32)
        hi, lo = split(v * v)
        return dot(ones, hi, 1, 1) + dot(ones, lo, 1, 1)

    sk = sketch_ref[...]
    own_norm = norms(sk[:, :512]) + norms(sk[:, 512:])

    pick(1)
    t_norm = norms(targ[0]) + norms(targ[1])
    dots = dot(sk[:, :512], targ[0], 1, 1) + dot(sk[:, 512:], targ[1], 1, 1)
    own_pad = jnp.concatenate([own_norm, jnp.zeros((8, NT - EX), F32)], axis=1)

    def pack(d, tn, on):
        thi, tlo = split(tn)
        ohi, olo = split(on)
        rr = iota((16, NT), 0)
        pick_row = lambda v: jnp.concatenate([v.astype(F32)] * 2, axis=0)
        tail = jnp.where(
            rr == 0, pick_row(thi), jnp.where(rr == 1, pick_row(tlo), jnp.where(rr == 2, pick_row(ohi), pick_row(olo)))
        )
        return jnp.concatenate([d, tail], axis=0).astype(BF)

    def m_copy(k):
        return remote(msg, mrx.at[k - 1], ms_sem.at[k - 1], mr_sem.at[k - 1], dev_x(k))

    msg[...] = pack(dots, t_norm, own_pad)
    for k in (2, 1, 3):
        m_copy(k).start()
    for k in range(1, NX):
        m_copy(k).wait_recv()
    total = (msg[...].astype(F32) + mrx[0].astype(F32)) + (mrx[1].astype(F32) + mrx[2].astype(F32))

    def unpack(m):
        return m[:EX], m[EX : EX + 1] + m[EX + 1 : EX + 2], m[EX + 2 : EX + 3] + m[EX + 3 : EX + 4]

    d, tn, on = unpack(total)
    mzs[...] = pack(d, jnp.broadcast_to(tn, (8, NT)), jnp.broadcast_to(on, (8, NT)))
    last = remote(mzs, mzr, fs_sem.at[0], fr_sem.at[0], dev_zh)
    last.start()
    last.wait_recv()
    d, tn, on = unpack(mzs[...].astype(F32) + mzr[...].astype(F32))
    diag = jnp.where(iota((EX, EX), 0) == iota((EX, EX), 1), on[:, :EX], 0.0)
    on_col = jnp.sum(diag, axis=1, keepdims=True)
    scores_ref[...] = math.sqrt(8192.0) * d * lax.rsqrt(on_col + 1e-6) * lax.rsqrt(tn + 1e-6)

    for n in range(CHUNKS):
        for k in range(1, NX):
            x_copy(n, k).wait_send()
        z_copy(n).wait_send()
    for k in range(1, NZL):
        zl_copy(k).wait_send()
    for g in range(2):
        for j in range(len(yc)):
            yc_copy(g, j).wait_send()
    for k in range(1, NX):
        m_copy(k).wait_send()
    last.wait_send()


def body(cotangent, low_acts, sign_bits, sample_blocks, bank, target_ids):
    any_spec = pl.BlockSpec(memory_space=pl.ANY)
    vmem = pl.BlockSpec(memory_space=pltpu.VMEM)
    dma = pltpu.SemaphoreType.DMA
    return pl.pallas_call(
        kernel,
        out_shape=(
            jax.ShapeDtypeStruct((EX, SHARE), BF),
            jax.ShapeDtypeStruct((EX, NT), F32),
        ),
        in_specs=[any_spec] * 6,
        out_specs=(vmem, vmem),
        scratch_shapes=[
            pltpu.VMEM((EX, TOK, ODEV), BF),
            pltpu.VMEM((EX, TOK, RANK), BF),
            pltpu.VMEM((3, ODEV), I32),
            pltpu.VMEM((1, NSAMP), I32),
            pltpu.VMEM((8, SHARE), BF),
            pltpu.VMEM((1, NT), I32),
            pltpu.VMEM((COLS, ODEV), BF),
            pltpu.VMEM((128, ODEV), BF),
            pltpu.VMEM((CHUNKS, 32, COLS), F32),
            pltpu.VMEM((CHUNKS, 3, 32, COLS), BF),
            pltpu.VMEM((CHUNKS, 3, 32, COLS), BF),
            pltpu.VMEM((CHUNKS, 16, COLS), F32),
            pltpu.VMEM((CHUNKS, 16, COLS), BF),
            pltpu.VMEM((CHUNKS, 16, COLS), BF),
            pltpu.VMEM((256, 128), F32),
            pltpu.VMEM((8, NZL, 16, 512), BF),
            pltpu.VMEM((2, NT, 512), BF),
            pltpu.VMEM((MSG, NT), BF),
            pltpu.VMEM((3, MSG, NT), BF),
            pltpu.VMEM((MSG, NT), BF),
            pltpu.VMEM((MSG, NT), BF),
            dma((6,)),
            dma((CHUNKS, 3)),
            dma((CHUNKS, 3)),
            dma((CHUNKS,)),
            dma((CHUNKS,)),
            dma((7,)),
            dma((7,)),
            dma((2, 7)),
            dma((2, 7)),
            dma((3,)),
            dma((3,)),
            dma((1,)),
            dma((1,)),
        ],
        compiler_params=pltpu.CompilerParams(
            collective_id=0, has_side_effects=True, vmem_limit_bytes=50 * 1024 * 1024
        ),
        name="sketch_scores",
    )(cotangent, low_acts, sign_bits.T, sample_blocks[None, :], bank, target_ids[None, :])


def solution(mesh):
    in_specs = (
        P("ex", None, "coord"),
        P("ex", None, None),
        P("coord", None),
        P(),
        P("ex", "coord"),
        P(),
    )
    out_specs = (P("ex", "coord"), P("ex", None))
    return jax.shard_map(body, mesh=mesh, in_specs=in_specs, out_specs=out_specs, check_vma=False)
```

time: 243 us -> 52.6 us (0.22)
  the two profiles are of different devices: /device:TPU:8 before, /device:TPU:96 now
where the time goes in v1:
time: 52.6 us; the launch traced here: 52.3 us
  Pallas kernels  45.1 us (86%)
  local copies, waits for them, and re-layouts  6.62 us (13%)
  between operations  0.65 us (1%)
    pallas_call x1, Pallas kernels, body(): pl.pallas_call(kernel, out_shape=(jax.ShapeDtypeStruct((EX, SHARE), BF),...  45.1 us
    unnamed x14, local copies, waits for them, and re-layouts  6.62 us

profile of v1, /device:TPU:96, one launch (start us, length us, event | category | flops | bytes accessed | tf_op | source)
XLA Modules:
  0.0 52.3 jit_solution(12255871225985641186)
XLA Ops:
  0.6 0.0 copy-start
  0.6 1.6 %copy-done = bf16[32,64,512]{2,1,0:T(8,128)(2,1)S(1)} copy-done((bf16[32,64,512]{2,1,0:T(8,128)(2,1)S(1)}, bf16[32,64,512]{2,1,0:T(8,128)(2,1)}, u32[]{:S(2)}) %copy-start) | copy-done | bytes 2097176
  2.2 0.0 copy-start.1
  2.2 1.0 %copy-done.1 = bf16[32,64,64]{2,1,0:T(8,128)(2,1)S(1)} copy-done((bf16[32,64,64]{2,1,0:T(8,128)(2,1)S(1)}, bf16[32,64,64]{2,1,0:T(8,128)(2,1)}, u32[]{:S(2)}) %copy-start.1) | copy-done | bytes 262168
  3.3 0.0 copy-start.2
  3.3 0.7 %copy-done.2 = bf16[8,1024]{1,0:T(8,128)(2,1)S(1)} copy-done((bf16[8,1024]{1,0:T(8,128)(2,1)S(1)}, bf16[8,1024]{1,0:T(8,128)(2,1)}, u32[]{:S(2)}) %copy-start.2) | copy-done | bytes 16408
  4.0 0.0 copy-start.3
  4.0 0.7 %copy-done.3 = s32[512,3]{0,1:T(4,128)S(1)} copy-done((s32[512,3]{0,1:T(4,128)S(1)}, s32[512,3]{0,1:T(4,128)}, u32[]{:S(2)}) %copy-start.3) | copy-done | bytes 6168
  4.7 0.0 copy-start.4
  4.7 0.7 %copy-done.4 = s32[256]{0:T(256)S(1)} copy-done((s32[256]{0:T(256)S(1)}, s32[256]{0:T(256)}, u32[]{:S(2)}) %copy-start.4) | copy-done | bytes 1048
  5.4 0.0 copy-start.5
  5.4 0.7 %copy-done.5 = s32[64]{0:T(128)S(1)} copy-done((s32[64]{0:T(128)S(1)}, s32[64]{0:T(128)}, u32[]{:S(2)}) %copy-start.5) | copy-done | bytes 280
  6.0 45.1 %sketch_scores.1 = (bf16[32,1024]{1,0:T(8,128)(2,1)S(1)}, f32[32,256]{1,0:T(8,128)S(1)}) custom-call(bf16[32,64,512]{2,1,0:T(8,128)(2,1)S(1)} %copy-done, bf16[32,64,64]{2,1,0:T(8,128)(2,1)S(1)} %copy-done.1, s32[3,512]{1,0:T(4,128)S(1)} %bitcast.3, s32[1,64]{1,0:T(1,128)S(1)} %bitcast.5, bf16[8,1024]{1,0:T(8,128)(2,1)S(1)} %copy-done.2, s32[1,256]{1,0:T(1,128)S(1)} %bitcast.4), custom_call_target="tpu_custom_call" | custom-call | tf_op jit(solution)/shard_map/sketch_scores/pallas_call | solution.py:288
  51.1 0.6 %copy.10 = bf16[32,1024]{1,0:T(8,128)(2,1)} copy(bf16[32,1024]{1,0:T(8,128)(2,1)S(1)} %get-tuple-element.4) | data formatting | bytes 131072
  51.7 0.6 %copy.11 = f32[32,256]{1,0:T(8,128)} copy(f32[32,256]{1,0:T(8,128)S(1)} %get-tuple-element.5) | data formatting | bytes 65536
Async XLA Ops:
  0.6 1.6 %copy-start = (bf16[32,64,512]{2,1,0:T(8,128)(2,1)S(1)}, bf16[32,64,512]{2,1,0:T(8,128)(2,1)}, u32[]{:S(2)}) copy-start(bf16[32,64,512]{2,1,0:T(8,128)(2,1)} %cot_hbm.1) | copy-start | bytes 6291460
  2.2 1.0 %copy-start.1 = (bf16[32,64,64]{2,1,0:T(8,128)(2,1)S(1)}, bf16[32,64,64]{2,1,0:T(8,128)(2,1)}, u32[]{:S(2)}) copy-start(bf16[32,64,64]{2,1,0:T(8,128)(2,1)} %low_hbm.1) | copy-start | bytes 786436
  3.3 0.7 %copy-start.2 = (bf16[8,1024]{1,0:T(8,128)(2,1)S(1)}, bf16[8,1024]{1,0:T(8,128)(2,1)}, u32[]{:S(2)}) copy-start(bf16[8,1024]{1,0:T(8,128)(2,1)} %bank_hbm.1) | copy-start | bytes 49156
  4.0 0.7 %copy-start.3 = (s32[512,3]{0,1:T(4,128)S(1)}, s32[512,3]{0,1:T(4,128)}, u32[]{:S(2)}) copy-start(s32[512,3]{0,1:T(4,128)} %param.8) | copy-start | bytes 18436
  4.7 0.7 %copy-start.4 = (s32[256]{0:T(256)S(1)}, s32[256]{0:T(256)}, u32[]{:S(2)}) copy-start(s32[256]{0:T(256)} %param.11) | copy-start | bytes 3076
  5.4 0.7 %copy-start.5 = (s32[64]{0:T(128)S(1)}, s32[64]{0:T(128)}, u32[]{:S(2)}) copy-start(s32[64]{0:T(128)} %param.9) | copy-start | bytes 772

commit v2 on v1

--- a/solution.py
+++ b/solution.py
@@ -64,7 +64,7 @@
     cot, low, sign, samp, bank, ids,
     st, had, part, xs, xr, own, zs, zr, ytmp, gath, targ, msg, mrx, mzs, mzr,
     in_sem, xs_sem, xr_sem, zs_sem, zr_sem, ls_sem, lr_sem, ys_sem, yr_sem,
-    ms_sem, mr_sem, fs_sem, fr_sem,
+    ms_sem, mr_sem, fs_sem, fr_sem, ready,
 ):
     ex, co = lax.axis_index("ex"), lax.axis_index("coord")
     c, zl, y = ex % 2, (ex // 2) % NZL, ex // (2 * NZL)
@@ -83,10 +83,18 @@
 
     barrier = pltpu.get_barrier_semaphore()
     yc = [(yk, ck) for yk in range(NY) for ck in range(2) if yk or ck]
-    partners = [dev_zh] + [dev_zl(k) for k in range(NZL - 1, 0, -1)]
-    partners += [dev_x(k) for k in range(1, NX)] + [dev_yc(*p) for p in yc]
-    for p in partners:
+    here = ex - c
+    sibling = (here + 1 - c, co)
+    far = [(here + 1, (1 - zh) * NX + x)]
+    near = [((y * NZL + xor(zl, k)) * 2, co) for k in (4, 3, 2, 1)]
+    near += [((xor(y, k) * NZL + zl) * 2, co) for k in range(1, NY)]
+    near += [(here, zh * NX + xor(x, k)) for k in range(1, NX)]
+    for p in far + near:
         pl.semaphore_signal(barrier, inc=1, device_id=p, device_id_type=MESH)
+
+    @pl.when(c == 1)
+    def _():
+        pl.semaphore_signal(barrier, inc=1, device_id=sibling, device_id_type=MESH)
 
     loads = [
         pltpu.make_async_copy(src, dst, in_sem.at[n])
@@ -132,7 +140,14 @@
 
     lax.fori_loop(0, CHUNKS, compute, 0)
 
-    pl.semaphore_wait(barrier, len(partners))
+    @pl.when(c == 0)
+    def _():
+        pl.semaphore_wait(barrier, 2 * len(near) + 1)
+        pl.semaphore_signal(ready, inc=1, device_id=sibling, device_id_type=MESH)
+
+    @pl.when(c == 1)
+    def _():
+        pl.semaphore_wait(ready, 1)
 
     def remote(src, dst, ssem, rsem, to):
         return pltpu.make_async_remote_copy(
@@ -146,18 +161,20 @@
         return remote(zs.at[n], zr.at[n], zs_sem.at[n], zr_sem.at[n], dev_zh)
 
     def zl_copy(k):
-        return remote(gath.at[0, 0], gath.at[0, k], ls_sem.at[k - 1], lr_sem.at[k - 1], dev_zl(k))
+        via = k if k <= 4 else k - 4
+        return remote(gath.at[0, k - via], gath.at[0, k], ls_sem.at[k - 1], lr_sem.at[k - 1], dev_zl(via))
 
     def yc_copy(g, j):
         yk, ck = yc[j]
         four = pl.ds(g * 4, 4)
-        return remote(gath.at[0, four], gath.at[j + 1, four], ys_sem.at[g, j], yr_sem.at[g, j], dev_yc(yk, ck))
-
-    for k in (2, 1, 3):
-        x_copy(0, k).start()
-    for k in range(NZL - 1, 0, -1):
+        to = sibling if ck else dev_yc(yk, 0)
+        return remote(
+            gath.at[yk * 2 if ck else 0, four], gath.at[j + 1, four], ys_sem.at[g, j], yr_sem.at[g, j], to
+        )
+
+    for k in (4, 3, 2, 1):
         zl_copy(k).start()
-    for n in range(1, CHUNKS):
+    for n in range(CHUNKS):
         for k in (2, 1, 3):
             x_copy(n, k).start()
 
@@ -169,21 +186,17 @@
         zs[n] = total[16:].astype(BF)
         z_copy(n).start()
 
-    def forward(g, first):
-        for k in range(first, g * 4 + 4):
-            zl_copy(k).wait_recv()
-        for j in range(len(yc) - 1, -1, -1):
+    def along_y(g):
+        for j in (3, 1, 5, 0):
             yc_copy(g, j).start()
 
-    x_done(0)
-    x_done(1)
-    forward(0, 1)
-    x_done(2)
-    x_done(3)
-    forward(1, 4)
+    def across(g):
+        for j in (1, 3, 5):
+            yc_copy(g, j).wait_recv()
+            yc_copy(g, j + 1).start()
 
     def pick(g):
-        for j in range(len(yc)):
+        for j in (0, 2, 4, 6):
             yc_copy(g, j).wait_recv()
         rows = 8 * 64
         lane = iota((rows, 1), 0)
@@ -200,7 +213,30 @@
             else:
                 targ[h] = (targ[h].astype(F32) + got).astype(BF)
 
+    zl_copy(4).wait_recv()
+    for k in (7, 6, 5):
+        zl_copy(k).start()
+    for k in (1, 2, 3):
+        zl_copy(k).wait_recv()
+    along_y(0)
+
+    @pl.when(c == 1)
+    def _():
+        pl.semaphore_wait(barrier, 2 * len(far))
+        pl.semaphore_signal(ready, inc=1, device_id=sibling, device_id_type=MESH)
+
+    @pl.when(c == 0)
+    def _():
+        pl.semaphore_wait(ready, 1)
+
+    for n in range(CHUNKS):
+        x_done(n)
+    for k in (5, 6, 7):
+        zl_copy(k).wait_recv()
+    along_y(1)
+    across(0)
     pick(0)
+    across(1)
 
     a, b = iota((128, 128), 0), iota((128, 128), 1)
     small = jnp.where((a // 64) == (b // 64), parity_sign(a & b & 63, 6), 0.0).astype(BF)
@@ -282,7 +318,7 @@
 
 
 def body(cotangent, low_acts, sign_bits, sample_blocks, bank, target_ids):
-    any_spec = pl.BlockSpec(memory_space=pl.ANY)
+    hbm = pl.BlockSpec(memory_space=pltpu.HBM)
     vmem = pl.BlockSpec(memory_space=pltpu.VMEM)
     dma = pltpu.SemaphoreType.DMA
     return pl.pallas_call(
@@ -291,7 +327,7 @@
             jax.ShapeDtypeStruct((EX, SHARE), BF),
             jax.ShapeDtypeStruct((EX, NT), F32),
         ),
-        in_specs=[any_spec] * 6,
+        in_specs=[hbm] * 6,
         out_specs=(vmem, vmem),
         scratch_shapes=[
             pltpu.VMEM((EX, TOK, ODEV), BF),
@@ -328,9 +364,10 @@
             dma((3,)),
             dma((1,)),
             dma((1,)),
+            pltpu.SemaphoreType.REGULAR,
         ],
         compiler_params=pltpu.CompilerParams(
-            collective_id=0, has_side_effects=True, vmem_limit_bytes=50 * 1024 * 1024
+            collective_id=0, has_side_effects=True, vmem_limit_bytes=60 * 1024 * 1024
         ),
         name="sketch_scores",
     )(cotangent, low_acts, sign_bits.T, sample_blocks[None, :], bank, target_ids[None, :])

time: 52.6 us -> 49.5 us (0.941)
  local copies, waits for them, and re-layouts: 6.62 us -> 2.85 us
  Pallas kernels: 45.1 us -> 45.7 us
    unnamed x14 -> x2, local copies, waits for them, and re-layouts: 6.62 us -> 2.85 us
    pallas_call x1, Pallas kernels: 45.1 us -> 45.7 us  [body(): pl.pallas_call(kernel, out_shape=(jax.ShapeDtypeStruct((EX, SHARE), BF),...]
where the time goes in v2:
time: 49.5 us; the launch traced here: 49.2 us
  Pallas kernels  45.7 us (92%)
  local copies, waits for them, and re-layouts  2.85 us (6%)
  between operations  0.64 us (1%)
    pallas_call x1, Pallas kernels, body(): pl.pallas_call(kernel, out_shape=(jax.ShapeDtypeStruct((EX, SHARE), BF),...  45.7 us
    unnamed x2, local copies, waits for them, and re-layouts  2.85 us

profile of v2, /device:TPU:96, one launch (start us, length us, event | category | flops | bytes accessed | tf_op | source)
XLA Modules:
  0.0 49.2 jit_solution(6700729279619521678)
XLA Ops:
  0.6 45.7 %sketch_scores.1 = (bf16[32,1024]{1,0:T(8,128)(2,1)}, f32[32,256]{1,0:T(8,128)}) custom-call(bf16[32,64,512]{2,1,0:T(8,128)(2,1)} %cot_hbm.1, bf16[32,64,64]{2,1,0:T(8,128)(2,1)} %low_hbm.1, s32[3,512]{1,0:T(4,128)} %bitcast.3, s32[1,64]{1,0:T(1,128)} %bitcast.5, bf16[8,1024]{1,0:T(8,128)(2,1)} %bank_hbm.1, s32[1,256]{1,0:T(1,128)} %bitcast.4), custom_call_target="tpu_custom_call" | custom-call | tf_op jit(solution)/shard_map/sketch_scores/pallas_call | solution.py:324
  46.4 1.5 %copy.10 = bf16[32,1024]{1,0:T(8,128)(2,1)} copy(bf16[32,1024]{1,0:T(8,128)(2,1)} %get-tuple-element.4) | data formatting | bytes 131072
  47.9 1.4 %copy.11 = f32[32,256]{1,0:T(8,128)} copy(f32[32,256]{1,0:T(8,128)} %get-tuple-element.5) | data formatting | bytes 65536

commit v3 on v2

--- a/solution.py
+++ b/solution.py
@@ -64,7 +64,7 @@
     cot, low, sign, samp, bank, ids,
     st, had, part, xs, xr, own, zs, zr, ytmp, gath, targ, msg, mrx, mzs, mzr,
     in_sem, xs_sem, xr_sem, zs_sem, zr_sem, ls_sem, lr_sem, ys_sem, yr_sem,
-    ms_sem, mr_sem, fs_sem, fr_sem, ready,
+    ms_sem, mr_sem, fs_sem, fr_sem,
 ):
     ex, co = lax.axis_index("ex"), lax.axis_index("coord")
     c, zl, y = ex % 2, (ex // 2) % NZL, ex // (2 * NZL)
@@ -83,18 +83,11 @@
 
     barrier = pltpu.get_barrier_semaphore()
     yc = [(yk, ck) for yk in range(NY) for ck in range(2) if yk or ck]
-    here = ex - c
-    sibling = (here + 1 - c, co)
-    far = [(here + 1, (1 - zh) * NX + x)]
-    near = [((y * NZL + xor(zl, k)) * 2, co) for k in (4, 3, 2, 1)]
-    near += [((xor(y, k) * NZL + zl) * 2, co) for k in range(1, NY)]
-    near += [(here, zh * NX + xor(x, k)) for k in range(1, NX)]
-    for p in far + near:
+    sibling = (ex + 1 - 2 * c, co)
+    partners = [dev_zh] + [dev_zl(k) for k in (4, 3, 2, 1)]
+    partners += [dev_yc(k, 0) for k in (2, 1, 3)] + [dev_x(k) for k in (2, 1, 3)] + [sibling]
+    for p in partners:
         pl.semaphore_signal(barrier, inc=1, device_id=p, device_id_type=MESH)
-
-    @pl.when(c == 1)
-    def _():
-        pl.semaphore_signal(barrier, inc=1, device_id=sibling, device_id_type=MESH)
 
     loads = [
         pltpu.make_async_copy(src, dst, in_sem.at[n])
@@ -139,15 +132,7 @@
         return 0
 
     lax.fori_loop(0, CHUNKS, compute, 0)
-
-    @pl.when(c == 0)
-    def _():
-        pl.semaphore_wait(barrier, 2 * len(near) + 1)
-        pl.semaphore_signal(ready, inc=1, device_id=sibling, device_id_type=MESH)
-
-    @pl.when(c == 1)
-    def _():
-        pl.semaphore_wait(ready, 1)
+    pl.semaphore_wait(barrier, len(partners))
 
     def remote(src, dst, ssem, rsem, to):
         return pltpu.make_async_remote_copy(
@@ -174,9 +159,12 @@
 
     for k in (4, 3, 2, 1):
         zl_copy(k).start()
-    for n in range(CHUNKS):
+    def x_start(n):
         for k in (2, 1, 3):
             x_copy(n, k).start()
+
+    for n in range(CHUNKS):
+        x_start(n)
 
     def x_done(n):
         for k in range(1, NX):
@@ -213,23 +201,14 @@
             else:
                 targ[h] = (targ[h].astype(F32) + got).astype(BF)
 
+    x_done(0)
     zl_copy(4).wait_recv()
     for k in (7, 6, 5):
         zl_copy(k).start()
     for k in (1, 2, 3):
         zl_copy(k).wait_recv()
     along_y(0)
-
-    @pl.when(c == 1)
-    def _():
-        pl.semaphore_wait(barrier, 2 * len(far))
-        pl.semaphore_signal(ready, inc=1, device_id=sibling, device_id_type=MESH)
-
-    @pl.when(c == 0)
-    def _():
-        pl.semaphore_wait(ready, 1)
-
-    for n in range(CHUNKS):
+    for n in range(1, CHUNKS):
         x_done(n)
     for k in (5, 6, 7):
         zl_copy(k).wait_recv()
@@ -364,7 +343,6 @@
             dma((3,)),
             dma((1,)),
             dma((1,)),
-            pltpu.SemaphoreType.REGULAR,
         ],
         compiler_params=pltpu.CompilerParams(
             collective_id=0, has_side_effects=True, vmem_limit_bytes=60 * 1024 * 1024

time: 49.5 us -> 48.4 us (0.978)
  the two profiles are of different devices: /device:TPU:96 before, /device:TPU:2 now
where the time goes in v3:
time: 48.4 us; the launch traced here: 48.1 us
  Pallas kernels  44.6 us (92%)
  local copies, waits for them, and re-layouts  2.85 us (6%)
  between operations  0.64 us (1%)
    pallas_call x1, Pallas kernels, body(): pl.pallas_call(kernel, out_shape=(jax.ShapeDtypeStruct((EX, SHARE), BF),...  44.6 us
    unnamed x2, local copies, waits for them, and re-layouts  2.85 us

profile of v3, /device:TPU:2, one launch (start us, length us, event | category | flops | bytes accessed | tf_op | source)
XLA Modules:
  0.0 48.1 jit_solution(16828116710028770660)
XLA Ops:
  0.6 44.6 %sketch_scores.1 = (bf16[32,1024]{1,0:T(8,128)(2,1)}, f32[32,256]{1,0:T(8,128)}) custom-call(bf16[32,64,512]{2,1,0:T(8,128)(2,1)} %cot_hbm.1, bf16[32,64,64]{2,1,0:T(8,128)(2,1)} %low_hbm.1, s32[3,512]{1,0:T(4,128)} %bitcast.3, s32[1,64]{1,0:T(1,128)} %bitcast.5, bf16[8,1024]{1,0:T(8,128)(2,1)} %bank_hbm.1, s32[1,256]{1,0:T(1,128)} %bitcast.4), custom_call_target="tpu_custom_call" | custom-call | tf_op jit(solution)/shard_map/sketch_scores/pallas_call | solution.py:303
  45.3 1.5 %copy.10 = bf16[32,1024]{1,0:T(8,128)(2,1)} copy(bf16[32,1024]{1,0:T(8,128)(2,1)} %get-tuple-element.4) | data formatting | bytes 131072
  46.7 1.4 %copy.11 = f32[32,256]{1,0:T(8,128)} copy(f32[32,256]{1,0:T(8,128)} %get-tuple-element.5) | data formatting | bytes 65536

commit v4 on v3

--- a/solution.py
+++ b/solution.py
@@ -205,10 +205,11 @@
     zl_copy(4).wait_recv()
     for k in (7, 6, 5):
         zl_copy(k).start()
+    x_done(1)
     for k in (1, 2, 3):
         zl_copy(k).wait_recv()
     along_y(0)
-    for n in range(1, CHUNKS):
+    for n in range(2, CHUNKS):
         x_done(n)
     for k in (5, 6, 7):
         zl_copy(k).wait_recv()

time: 48.4 us -> 48.4 us (level)
  no operation moved by 1% of the time
where the time goes in v4:
time: 48.4 us; the launch traced here: 48.1 us
  Pallas kernels  44.6 us (92%)
  local copies, waits for them, and re-layouts  2.85 us (6%)
  between operations  0.64 us (1%)
    pallas_call x1, Pallas kernels, body(): pl.pallas_call(kernel, out_shape=(jax.ShapeDtypeStruct((EX, SHARE), BF),...  44.6 us
    unnamed x2, local copies, waits for them, and re-layouts  2.85 us

profile of v4, /device:TPU:2, one launch (start us, length us, event | category | flops | bytes accessed | tf_op | source)
XLA Modules:
  0.0 48.1 jit_solution(4508830167069796901)
XLA Ops:
  0.6 44.6 %sketch_scores.1 = (bf16[32,1024]{1,0:T(8,128)(2,1)}, f32[32,256]{1,0:T(8,128)}) custom-call(bf16[32,64,512]{2,1,0:T(8,128)(2,1)} %cot_hbm.1, bf16[32,64,64]{2,1,0:T(8,128)(2,1)} %low_hbm.1, s32[3,512]{1,0:T(4,128)} %bitcast.3, s32[1,64]{1,0:T(1,128)} %bitcast.5, bf16[8,1024]{1,0:T(8,128)(2,1)} %bank_hbm.1, s32[1,256]{1,0:T(1,128)} %bitcast.4), custom_call_target="tpu_custom_call" | custom-call | tf_op jit(solution)/shard_map/sketch_scores/pallas_call | solution.py:304
  45.3 1.5 %copy.10 = bf16[32,1024]{1,0:T(8,128)(2,1)} copy(bf16[32,1024]{1,0:T(8,128)(2,1)} %get-tuple-element.4) | data formatting | bytes 131072
  46.7 1.4 %copy.11 = f32[32,256]{1,0:T(8,128)} copy(f32[32,256]{1,0:T(8,128)} %get-tuple-element.5) | data formatting | bytes 65536
